TPU v7x, 32 devices: a whole 2x2x4 slice. The times are simulated.
32 devices in a mesh: groups: 2 (over y), seq: 4 (over z), blk: 2 (over x), cfg: 2 (over core).
Axes of the slice: x: 2, y: 2, z: 4, core: 2. Of those that a mesh axis runs over, the one named last changes fastest.
Arguments:
- queries: bfloat16 [4, 320, 4096], P(('groups', 'cfg'), ('seq', 'blk')), parts along dimension 0, may hold values from -6 to 6
- keys: bfloat16 [4, 320, 4096], P(('groups', 'cfg'), ('seq', 'blk')), parts along dimension 0, may hold values from -6 to 6
- values: bfloat16 [4, 320, 4096], P(('groups', 'cfg'), ('seq', 'blk')), parts along dimension 0, may hold values from -6 to 6
- ref_keys: bfloat16 [4, 1024, 4096], P(('groups', 'cfg'), 'seq'), parts along dimension 0, may hold values from -6 to 6
- ref_values: bfloat16 [4, 1024, 4096], P(('groups', 'cfg'), 'seq'), parts along dimension 0, may hold values from -6 to 6
- ref_len: int32 [4], P(('groups', 'cfg')), parts along dimension 0, may hold values from 256 to 1024, as said below
- step_index: int32 [2], P('groups'), parts along dimension 0, may hold values from 0 to 49
- guide: float32 [2], P('groups'), parts along dimension 0, may hold values from 3 to 6
- latent: float32 [320, 128], P(('groups', 'seq', 'blk', 'cfg')), parts along dimension 0, may hold values from -6 to 6
- w_out: bfloat16 [4096, 64], replicated, may hold values from -1 to 1
Outputs:
- latent_next: float32 [320, 128], P(('groups', 'seq', 'blk', 'cfg')), parts along dimension 0
- denoised: float32 [320, 128], P(('groups', 'seq', 'blk', 'cfg')), parts along dimension 0
There are 2 independent parts, one for each index of `groups`. A program takes and returns all parts, laid end to end along the dimension named above; an argument that names none is the same for every part. Nothing has to cross between parts.
Inputs may be any that keep to these rules, and one draw needn't show every extreme that they name: `ref_len`: one of the two branches has exactly 1024 valid reference tokens.
All inputs are finite; a program needn't handle non-finite values.
Results may differ from a plain program's by a relative error of at most 0.005.
Values may be sent and summed in bfloat16 or wider, within the bound.
A program may use at most 128 MiB of HBM per device.

v0:
```python
from functools import partial

import jax
import jax.numpy as jnp
from jax import lax
from jax.sharding import PartitionSpec as P

HD = 128
STEPS = 50


def partner_2(value, axis, distance):
    mask = 2**distance
    pairs = [(source, source ^ mask) for source in range(lax.axis_size(axis))]
    return lax.ppermute(value, axis, pairs)


def fold_keys(query_block, carry, piece, start):
    top_old, total_old, accum = carry
    key_piece, value_piece = piece
    count = key_piece.shape[0]
    heads_here = query_block.shape[1]
    key_piece = key_piece.reshape(count, heads_here, HD)
    value_piece = value_piece.reshape(count, heads_here, HD)
    scores = jnp.einsum(
        "rhd,phd->rhp", query_block, key_piece, preferred_element_type=jnp.float32
    ) * HD ** (-0.5)
    top_new = jnp.maximum(top_old, jnp.max(scores, axis=2))
    weights = jnp.exp(scores - top_new[..., None])
    rescale = jnp.exp(top_old - top_new)
    total_new = jnp.sum(weights, axis=2)
    accum = jnp.einsum(
        "rhp,phd->rhd",
        weights.astype(jnp.bfloat16),
        value_piece,
        preferred_element_type=jnp.float32,
    )
    return (top_new, total_new, accum)


def reference_part(query_block, refkey_all, refvalue_all, length):
    count = refkey_all.shape[0]
    heads_here = query_block.shape[1]
    refkey_all = refkey_all.reshape(count, heads_here, HD)
    refvalue_all = refvalue_all.reshape(count, heads_here, HD)
    scores = jnp.einsum(
        "rhd,phd->rhp", query_block, refkey_all, preferred_element_type=jnp.float32
    ) * HD ** (-0.5)
    ref_index = jnp.arange(count, dtype=jnp.int32)[None, None, :]
    scores = jnp.where(ref_index < length, scores, jnp.float32(-1e30))
    top_score = jnp.max(scores, axis=2, keepdims=True)
    weights = jnp.exp(scores - top_score)
    summed = jnp.einsum(
        "rhp,phd->rhd",
        weights.astype(jnp.bfloat16),
        refvalue_all,
        preferred_element_type=jnp.float32,
    )
    return summed / jnp.sum(weights, axis=2)[..., None]


def attend_heads(query_rows, key_rows, value_rows, refkey_all, refvalue_all, length, gather_keys):
    rows_here = query_rows.shape[0]
    heads_here = query_rows.shape[1] // HD
    query_block = query_rows.reshape(rows_here, heads_here, HD)
    start_carry = (
        jnp.full((rows_here, heads_here), -1e30, jnp.float32),
        jnp.zeros((rows_here, heads_here), jnp.float32),
        jnp.zeros((rows_here, heads_here, HD), jnp.float32),
    )
    top_score, total, accum = gather_keys(
        partial(fold_keys, query_block), start_carry, key_rows, value_rows
    )
    combined = accum / total[..., None] + reference_part(
        query_block, refkey_all, refvalue_all, length
    )
    return combined.reshape(rows_here, heads_here * HD).astype(jnp.bfloat16)


def sigma_of(index):
    frac = 1.0 - index.astype(jnp.float32) / STEPS
    return 5.0 * frac / (1.0 + 4.0 * frac)


def on_device(
    queries, keys, values, ref_keys, ref_values, ref_len, step_index, guide, latent, w_out
):
    query_local = queries[0]
    key_local = keys[0]
    value_local = values[0]
    length = ref_len[0]
    query_rows, key_rows, value_rows = (
        lax.all_to_all(query_local, "seq", split_axis=1, concat_axis=0, tiled=True),
        lax.all_to_all(key_local, "seq", split_axis=1, concat_axis=0, tiled=True),
        lax.all_to_all(value_local, "seq", split_axis=1, concat_axis=0, tiled=True),
    )
    refkey_all, refvalue_all = (
        lax.all_to_all(ref_keys[0], "seq", split_axis=1, concat_axis=0, tiled=True),
        lax.all_to_all(ref_values[0], "seq", split_axis=1, concat_axis=0, tiled=True),
    )

    def gather_keys(step_fn, start_carry, key_rows, value_rows):
        return step_fn(
            start_carry,
            (
                lax.all_gather(key_rows, "blk", axis=0, tiled=True),
                lax.all_gather(value_rows, "blk", axis=0, tiled=True),
            ),
            jnp.int32(0),
        )

    attended = attend_heads(
        query_rows, key_rows, value_rows, refkey_all, refvalue_all, length, gather_keys
    )
    attended = lax.all_to_all(attended, "seq", split_axis=0, concat_axis=1, tiled=True)
    velocity = jnp.dot(attended, w_out, preferred_element_type=jnp.float32)
    pair_rows = velocity.shape[0] // 2
    velocity = velocity.reshape(pair_rows, 2 * velocity.shape[1])
    half_rows = pair_rows // 2
    branch = lax.axis_index("cfg")
    scale_now = guide[0]
    partner = partner_2(velocity, "cfg", 0)
    cond_vel = jnp.where(branch == 0, velocity, partner)
    uncond_vel = jnp.where(branch == 0, partner, velocity)
    guided = uncond_vel + scale_now * (cond_vel - uncond_vel)
    guided = lax.dynamic_slice_in_dim(guided, branch * half_rows, half_rows, 0)
    sig_now = sigma_of(step_index[0])
    sig_next = sigma_of(step_index[0] + 1)
    latent_next = latent + (sig_next - sig_now) * guided
    denoised = latent - sig_now * guided
    return (latent_next, denoised)


def solution(mesh):
    in_specs = (
        P(("groups", "cfg"), ("seq", "blk"), None),
        P(("groups", "cfg"), ("seq", "blk"), None),
        P(("groups", "cfg"), ("seq", "blk"), None),
        P(("groups", "cfg"), "seq", None),
        P(("groups", "cfg"), "seq", None),
        P(("groups", "cfg")),
        P("groups"),
        P("groups"),
        P(("groups", "seq", "blk", "cfg"), None),
        P(),
    )
    out_specs = (P(("groups", "seq", "blk", "cfg"), None), P(("groups", "seq", "blk", "cfg"), None))
    return jax.shard_map(
        on_device, mesh=mesh, in_specs=in_specs, out_specs=out_specs, check_vma=False
    )
```

profile of v0, /device:TPU:0, one launch (start us, length us, event | category | flops | bytes accessed | tf_op | source)
XLA Modules:
  0.0 165.5 jit_solution(1815150250300368351)
XLA Ops:
  0.6 0.0 copy-start
  0.6 0.0 copy-start.6
  0.7 0.0 copy-start.7
  0.7 1.3 all_to_all.80
  2.0 0.8 copy.37
  2.8 6.3 %all-to-all-start.1 = ((bf16[40,4,1024]{2,0,1:T(8,128)(2,1)}), bf16[40,4,1024]{2,0,1:T(8,128)(2,1)S(1)}, u32[]{:S(2)}, u32[]{:S(2)}) async-start(bf16[40,4,1024]{2,0,1:T(8,128)(2,1)} %copy.37), calls=%async_computation.1 | async-start | bytes 655360 | tf_op jit(solution)/shard_map/all_to_all | solution.py:93
  9.1 0.2 all_to_all.76
  9.3 0.8 copy.36
  10.2 9.3 %all-to-all-done.1 = bf16[40,4,1024]{2,0,1:T(8,128)(2,1)S(1)} async-done(((bf16[40,4,1024]{2,0,1:T(8,128)(2,1)}), bf16[40,4,1024]{2,0,1:T(8,128)(2,1)S(1)}, u32[]{:S(2)}, u32[]{:S(2)}) %all-to-all-start.1) | async-done | bytes 327712 | tf_op jit(solution)/shard_map/all_to_all | solution.py:93
  19.4 3.5 %all-to-all-start = ((bf16[40,4,1024]{2,0,1:T(8,128)(2,1)}), bf16[40,4,1024]{2,0,1:T(8,128)(2,1)S(1)}, u32[]{:S(2)}, u32[]{:S(2)}) async-start(bf16[40,4,1024]{2,0,1:T(8,128)(2,1)} %copy.36), calls=%async_computation | async-start | bytes 655360 | tf_op jit(solution)/shard_map/all_to_all | solution.py:94
  22.9 0.2 all_to_all.83
  23.1 0.8 copy.40
  24.0 7.5 %all-to-all-done = bf16[40,4,1024]{2,0,1:T(8,128)(2,1)S(1)} async-done(((bf16[40,4,1024]{2,0,1:T(8,128)(2,1)}), bf16[40,4,1024]{2,0,1:T(8,128)(2,1)S(1)}, u32[]{:S(2)}, u32[]{:S(2)}) %all-to-all-start) | async-done | bytes 327712 | tf_op jit(solution)/shard_map/all_to_all | solution.py:94
  31.5 4.1 %all-to-all-start.2 = ((bf16[40,4,1024]{2,0,1:T(8,128)(2,1)}), bf16[40,4,1024]{2,0,1:T(8,128)(2,1)}, u32[]{:S(2)}, u32[]{:S(2)}) async-start(bf16[40,4,1024]{2,0,1:T(8,128)(2,1)} %copy.40), calls=%async_computation.2 | async-start | bytes 655360 | tf_op jit(solution)/shard_map/all_to_all | solution.py:95
  35.6 3.3 %all_to_all.90 = bf16[256,4,1024]{2,1,0:T(4,128)(2,1)S(1)} reshape(bf16[1,256,4096]{2,1,0:T(8,128)(2,1)} %param.14) | data formatting | bytes 4194304 | tf_op jit(solution)/shard_map/all_to_all | solution.py:99
  38.9 1.9 %copy.45 = bf16[256,4,1024]{2,0,1:T(8,128)(2,1)} copy(bf16[256,4,1024]{2,1,0:T(4,128)(2,1)S(1)} %all_to_all.90) | data formatting | bytes 4194304 | tf_op jit(solution)/shard_map/all_to_all | solution.py:99
  40.9 2.1 %all-to-all-done.2 = bf16[40,4,1024]{2,0,1:T(8,128)(2,1)} async-done(((bf16[40,4,1024]{2,0,1:T(8,128)(2,1)}), bf16[40,4,1024]{2,0,1:T(8,128)(2,1)}, u32[]{:S(2)}, u32[]{:S(2)}) %all-to-all-start.2) | async-done | bytes 327712 | tf_op jit(solution)/shard_map/all_to_all | solution.py:95
  43.0 3.6 %all-to-all-start.4 = ((bf16[256,4,1024]{2,0,1:T(8,128)(2,1)}), bf16[256,4,1024]{2,0,1:T(8,128)(2,1)S(1)}, u32[]{:S(2)}, u32[]{:S(2)}) async-start(bf16[256,4,1024]{2,0,1:T(8,128)(2,1)} %copy.45), calls=%async_computation.4 | async-start | bytes 4194304 | tf_op jit(solution)/shard_map/all_to_all | solution.py:99
  46.6 4.5 %all_to_all.87 = bf16[256,4,1024]{2,1,0:T(4,128)(2,1)} reshape(bf16[1,256,4096]{2,1,0:T(8,128)(2,1)} %param.13) | data formatting | bytes 4194304 | tf_op jit(solution)/shard_map/all_to_all | solution.py:98
  51.1 3.6 %copy.42 = bf16[256,4,1024]{2,0,1:T(8,128)(2,1)} copy(bf16[256,4,1024]{2,1,0:T(4,128)(2,1)} %all_to_all.87) | data formatting | bytes 4194304 | tf_op jit(solution)/shard_map/all_to_all | solution.py:98
  54.6 36.2 %all-to-all-done.4 = bf16[256,4,1024]{2,0,1:T(8,128)(2,1)S(1)} async-done(((bf16[256,4,1024]{2,0,1:T(8,128)(2,1)}), bf16[256,4,1024]{2,0,1:T(8,128)(2,1)S(1)}, u32[]{:S(2)}, u32[]{:S(2)}) %all-to-all-start.4) | async-done | bytes 2097184 | tf_op jit(solution)/shard_map/all_to_all | solution.py:99
  90.8 4.4 %all-to-all-start.3 = ((bf16[256,4,1024]{2,0,1:T(8,128)(2,1)}), bf16[256,4,1024]{2,0,1:T(8,128)(2,1)}, u32[]{:S(2)}, u32[]{:S(2)}) async-start(bf16[256,4,1024]{2,0,1:T(8,128)(2,1)} %copy.42), calls=%async_computation.3 | async-start | bytes 4194304 | tf_op jit(solution)/shard_map/all_to_all | solution.py:98
  95.9 0.1 copy.52
  96.0 9.3 %all_gather.6 = bf16[320,1024]{1,0:T(8,128)(2,1)S(1)} all-gather(bf16[160,1024]{1,0:T(8,128)(2,1)S(1)} %bitcast.87), channel_id=1, replica_groups=mesh['groups'=2,'seq'=4,'blk'=2,'cfg'=2] {'blk'}, dimensions={0}, use_global_device_ids=true | all-gather | bytes 983040 | tf_op jit(solution)/shard_map/all_gather | solution.py:106
  105.4 8.7 %all_gather.7 = bf16[320,1024]{1,0:T(8,128)(2,1)S(1)} all-gather(bf16[160,1024]{1,0:T(8,128)(2,1)} %bitcast.7), channel_id=1, replica_groups=mesh['groups'=2,'seq'=4,'blk'=2,'cfg'=2] {'blk'}, dimensions={0}, use_global_device_ids=true | all-gather | bytes 983040 | tf_op jit(solution)/shard_map/all_gather | solution.py:107
  114.1 0.6 bitcast_reduce_fusion.1
  114.7 1.3 copy-done.1
  115.9 0.8 fusion.13
  116.7 2.0 %copy.54 = bf16[128,8,8,128]{3,2,1,0:T(8,128)(2,1)} copy(bf16[128,8,8,128]{3,1,2,0:T(8,128)(2,1)S(1)} %bitcast.81) | data formatting | bytes 4194304
  118.7 24.4 %all-to-all-done.3 = bf16[256,4,1024]{2,0,1:T(8,128)(2,1)} async-done(((bf16[256,4,1024]{2,0,1:T(8,128)(2,1)}), bf16[256,4,1024]{2,0,1:T(8,128)(2,1)}, u32[]{:S(2)}, u32[]{:S(2)}) %all-to-all-start.3) | async-done | bytes 2097184 | tf_op jit(solution)/shard_map/all_to_all | solution.py:98
  143.0 2.3 %copy.53 = bf16[128,8,8,128]{3,2,1,0:T(8,128)(2,1)S(1)} copy(bf16[128,8,8,128]{3,1,2,0:T(8,128)(2,1)} %bitcast.28) | data formatting | bytes 4194304
  145.3 0.0 copy-done.5
  145.3 1.2 bitcast_reduce_fusion
  146.5 1.3 fusion.1
  147.8 0.3 copy-done.3
  148.1 1.8 %fusion.23 = f32[160,8,128]{2,0,1:T(8,128)S(1)} fusion(bf16[1024,8,128]{2,1,0:T(8,128)(2,1)S(1)} %bitcast.82, f32[8,1024,160]{1,2,0:T(8,128)S(1)} %get-tuple-element.5, f32[160,8]{0,1:T(8,128)S(1)} %get-tuple-element.4, pred[1024]{0:T(1024)(128)(4,1)S(1)} %iota_compare_fusion, f32[160,8]{0,1:T(8,128)S(1)} %fusion.1), kind=kOutput, calls=%fused_computation.24 | convolution fusion | flops 340951040 | bytes 8006656 | tf_op jit(solution)/shard_map/rhp,phd->rhd/dot_general | solution.py:53
  149.9 0.8 fusion.22
  150.6 0.0 copy-start.8
  150.6 0.1 copy.47
  150.8 0.1 convert_element_type.26
  150.9 12.1 %all_to_all.102 = bf16[4,40,1024]{2,1,0:T(8,128)(2,1)S(1)} all-to-all(bf16[4,40,1024]{2,1,0:T(8,128)(2,1)S(1)} %convert_element_type.26), channel_id=1, replica_groups=mesh['groups'=2,'seq'=4,'blk'=2,'cfg'=2] {'seq'}, dimensions={0} | all-to-all | bytes 655360 | tf_op jit(solution)/shard_map/all_to_all | solution.py:115
  163.1 0.0 copy-done
  163.1 0.3 fusion.41
  163.4 0.1 reshape.83
  163.4 0.0 collective-permute-start
  164.9 0.0 collective-permute-done
  164.9 0.0 copy-done.8
  164.9 0.6 multiply_subtract_fusion
  (12 shorter events, 0.0 us)
Async XLA Ops:
  0.6 162.4 %copy-start = (bf16[4096,64]{0,1:T(8,128)(2,1)S(1)}, bf16[4096,64]{0,1:T(8,128)(2,1)}, u32[]{:S(2)}) copy-start(bf16[4096,64]{0,1:T(8,128)(2,1)} %param.19) | copy-start | bytes 1572868
  0.6 8.5 %copy-start.6 = (bf16[1,40,4096]{2,1,0:T(8,128)(2,1)S(1)}, bf16[1,40,4096]{2,1,0:T(8,128)(2,1)}, u32[]{:S(2)}) copy-start(bf16[1,40,4096]{2,1,0:T(8,128)(2,1)} %param.11) | copy-start | bytes 983044
  0.7 22.2 %copy-start.7 = (bf16[1,40,4096]{2,1,0:T(8,128)(2,1)S(1)}, bf16[1,40,4096]{2,1,0:T(8,128)(2,1)}, u32[]{:S(2)}) copy-start(bf16[1,40,4096]{2,1,0:T(8,128)(2,1)} %param.12) | copy-start | bytes 983044
  2.8 16.6 %all-to-all-start.1 = ((bf16[40,4,1024]{2,0,1:T(8,128)(2,1)}), bf16[40,4,1024]{2,0,1:T(8,128)(2,1)S(1)}, u32[]{:S(2)}, u32[]{:S(2)}) async-start(bf16[40,4,1024]{2,0,1:T(8,128)(2,1)} %copy.37), calls=%async_computation.1 | async-start | bytes 655360 | tf_op jit(solution)/shard_map/all_to_all | solution.py:93
  19.4 12.1 %all-to-all-start = ((bf16[40,4,1024]{2,0,1:T(8,128)(2,1)}), bf16[40,4,1024]{2,0,1:T(8,128)(2,1)S(1)}, u32[]{:S(2)}, u32[]{:S(2)}) async-start(bf16[40,4,1024]{2,0,1:T(8,128)(2,1)} %copy.36), calls=%async_computation | async-start | bytes 655360 | tf_op jit(solution)/shard_map/all_to_all | solution.py:94
  31.5 11.5 %all-to-all-start.2 = ((bf16[40,4,1024]{2,0,1:T(8,128)(2,1)}), bf16[40,4,1024]{2,0,1:T(8,128)(2,1)}, u32[]{:S(2)}, u32[]{:S(2)}) async-start(bf16[40,4,1024]{2,0,1:T(8,128)(2,1)} %copy.40), calls=%async_computation.2 | async-start | bytes 655360 | tf_op jit(solution)/shard_map/all_to_all | solution.py:95
  43.0 47.9 %all-to-all-start.4 = ((bf16[256,4,1024]{2,0,1:T(8,128)(2,1)}), bf16[256,4,1024]{2,0,1:T(8,128)(2,1)S(1)}, u32[]{:S(2)}, u32[]{:S(2)}) async-start(bf16[256,4,1024]{2,0,1:T(8,128)(2,1)} %copy.45), calls=%async_computation.4 | async-start | bytes 4194304 | tf_op jit(solution)/shard_map/all_to_all | solution.py:99
  90.8 52.2 %all-to-all-start.3 = ((bf16[256,4,1024]{2,0,1:T(8,128)(2,1)}), bf16[256,4,1024]{2,0,1:T(8,128)(2,1)}, u32[]{:S(2)}, u32[]{:S(2)}) async-start(bf16[256,4,1024]{2,0,1:T(8,128)(2,1)} %copy.42), calls=%async_computation.3 | async-start | bytes 4194304 | tf_op jit(solution)/shard_map/all_to_all | solution.py:98
  96.0 18.6 %copy-start.4 = (bf16[20,8,8,128]{3,2,1,0:T(8,128)(2,1)}, bf16[20,8,8,128]{3,2,1,0:T(8,128)(2,1)S(1)}, u32[]{:S(2)}) copy-start(bf16[20,8,8,128]{3,2,1,0:T(8,128)(2,1)S(1)} %copy.52) | copy-start | bytes 983044
  114.6 1.3 copy-start.1
  143.0 2.3 %copy-start.5 = (bf16[20,8,8,128]{3,2,1,0:T(8,128)(2,1)S(1)}, bf16[20,8,8,128]{3,2,1,0:T(8,128)(2,1)}, u32[]{:S(2)}) copy-start(bf16[20,8,8,128]{3,2,1,0:T(8,128)(2,1)} %copy-done.4) | copy-start | bytes 983044
  146.5 1.6 copy-start.3
  148.1 1.8 %copy-start.2 = (f32[8,320,160]{1,2,0:T(8,128)S(1)}, f32[8,320,160]{1,2,0:T(8,128)}, u32[]{:S(2)}) copy-start(f32[8,320,160]{1,2,0:T(8,128)} %copy-done.1) | copy-start | bytes 4915204
  150.6 14.3 %copy-start.8 = (f32[10,128]{1,0:T(8,128)S(1)}, f32[10,128]{1,0:T(8,128)}, u32[]{:S(2)}) copy-start(f32[10,128]{1,0:T(8,128)} %param.18) | copy-start | bytes 15364
  163.4 1.4 collective-permute-start
where the time goes:
time: 166 us
  waiting for transfers between devices  79.5 us (48%)
  blocking collectives  30.2 us (18%)
  local copies, waits for them, and re-layouts  23.8 us (14%)
  starting transfers between devices  21.9 us (13%)
  matrix products  4.52 us (3%)
  between operations  2.92 us (2%)
  other arithmetic  2.72 us (2%)
    all_to_all x1, waiting for transfers between devices, on_device(): lax.all_to_all(ref_values[0], 'seq', split_axis=1, concat_axis=0, tiled=T...  36.2 us
    all_to_all x1, waiting for transfers between devices, on_device(): lax.all_to_all(ref_keys[0], 'seq', split_axis=1, concat_axis=0, tiled=True)  24.4 us
    all_to_all x1, blocking collectives, on_device(): lax.all_to_all(attended, 'seq', split_axis=0, concat_axis=1, tiled=True)  12.1 us
    all_gather x1, blocking collectives, gather_keys(): lax.all_gather(key_rows, 'blk', axis=0, tiled=True)  9.34 us
    all_to_all x1, waiting for transfers between devices, on_device(): lax.all_to_all(query_local, 'seq', split_axis=1, concat_axis=0, tiled=True)  9.26 us
    all_gather x1, blocking collectives, gather_keys(): lax.all_gather(value_rows, 'blk', axis=0, tiled=True)  8.72 us
    all_to_all x2, local copies, waits for them, and re-layouts, on_device(): lax.all_to_all(ref_keys[0], 'seq', split_axis=1, concat_axis=0, tiled=True)  8.04 us
    all_to_all x1, waiting for transfers between devices, on_device(): lax.all_to_all(key_local, 'seq', split_axis=1, concat_axis=0, tiled=True)  7.53 us
  transfers between devices with their start and end apart: 6, of which 5 were waited for; matrix products, arithmetic and copies ran while one was open for 6% of the time, Pallas kernels for 0%

commit v1 on v0

v1 whole, which is shorter than its diff:
```python
import functools
import math

import jax
import jax.numpy as jnp
from jax import lax
from jax.experimental import pallas as pl
from jax.experimental.pallas import tpu as pltpu
from jax.sharding import PartitionSpec as P

HD = 128
STEPS = 50
FACTOR = HD ** (-0.5) * math.log2(math.e)
MESH = pl.DeviceIdType.MESH
BF16 = jnp.bfloat16
F32 = jnp.float32


def round_up(value, unit):
    return (value + unit - 1) // unit * unit


def sigma_of(frac_index):
    frac = 1.0 - frac_index / STEPS
    return 5.0 * frac / (1.0 + 4.0 * frac)


def dot_t(a, b):
    return lax.dot_general(a, b, (((1,), (1,)), ((), ())), preferred_element_type=F32)


def step_kernel(
    n,
    nx,
    nc,
    len_ref,
    step_ref,
    guide_ref,
    q_ref,
    k_ref,
    v_ref,
    rk_ref,
    rv_ref,
    w_ref,
    latent_ref,
    next_ref,
    denoised_ref,
    qbuf,
    kbuf,
    vbuf,
    rkey,
    rval,
    wraw,
    wdup,
    kself,
    vself,
    oref,
    oself,
    mstat,
    lstat,
    lse,
    att,
    vtmp,
    slab,
    landed,
    local_sem,
    x_send,
    q_recv,
    kv_recv,
    z_send,
    s_send,
    s_recv,
    v_send,
    v_recv,
):
    z = lax.axis_index("seq")
    x = lax.axis_index("blk")
    c = lax.axis_index("cfg")
    rows = q_ref.shape[1]
    width = qbuf.shape[3]
    heads = width // HD
    block = nx * rows
    padded = lse.shape[3]
    lanes_used = lse.shape[2]
    half = latent_ref.shape[0]
    refs = rkey.shape[0]

    def cols(index):
        return pl.ds(pl.multiple_of(index * width, HD), width)

    loads = [
        pltpu.make_async_copy(q_ref.at[0, :, cols(x)], qbuf.at[z, x], local_sem.at[0]),
        pltpu.make_async_copy(rk_ref.at[0, :, cols(x)], rkey, local_sem.at[1]),
        pltpu.make_async_copy(rv_ref.at[0, :, cols(x)], rval, local_sem.at[2]),
        pltpu.make_async_copy(k_ref.at[0, :, cols(x)], kbuf.at[x], local_sem.at[3]),
        pltpu.make_async_copy(v_ref.at[0, :, cols(x)], vbuf.at[x], local_sem.at[4]),
        pltpu.make_async_copy(
            w_ref.at[pl.ds(pl.multiple_of(x * width, HD), width), :], wraw, local_sem.at[5]
        ),
    ]
    for load in loads:
        load.start()

    members = n * nx * nc
    me = (z * nx + x) * nc + c

    def coords(index):
        return {"seq": index // (nx * nc), "blk": (index // nc) % nx, "cfg": index % nc}

    barrier = pltpu.get_barrier_semaphore()

    def greet(offset, carry):
        pl.semaphore_signal(
            barrier, inc=1, device_id=coords((me + offset) % members), device_id_type=MESH
        )
        return carry

    lax.fori_loop(1, members, greet, 0)
    pl.semaphore_wait(barrier, members - 1)

    def x_copy(offset, kind):
        source = (q_ref, k_ref, v_ref)[kind]
        target = (qbuf.at[z, x], kbuf.at[x], vbuf.at[x])[kind]
        arrived = (q_recv.at[z, x], kv_recv.at[0, x], kv_recv.at[1, x])[kind]
        to = (x + offset) % nx
        return pltpu.make_async_remote_copy(
            src_ref=source.at[0, :, cols(to)],
            dst_ref=target,
            send_sem=x_send.at[kind, offset],
            recv_sem=arrived,
            device_id={"blk": to},
            device_id_type=MESH,
        )

    def z_copy(side, b, piece):
        return pltpu.make_async_remote_copy(
            src_ref=qbuf.at[b, piece],
            dst_ref=qbuf.at[b, piece],
            send_sem=z_send.at[side, b, piece],
            recv_sem=q_recv.at[b, piece],
            device_id={"seq": z + 1 - 2 * side},
            device_id_type=MESH,
        )

    def forward(side, b, piece):
        @pl.when((z < n - 1) if side == 0 else (z > 0))
        def _():
            z_copy(side, b, piece).start()

    def arrived_q(b, piece):
        pltpu.make_async_remote_copy(
            src_ref=qbuf.at[b, piece],
            dst_ref=qbuf.at[b, piece],
            send_sem=z_send.at[0, b, piece],
            recv_sem=q_recv.at[b, piece],
            device_id={"blk": (x + 1) % nx},
            device_id_type=MESH,
        ).wait_recv()

    for kind in range(3):
        for offset in range(1, nx):
            x_copy(offset, kind).start()
    loads[0].wait()
    forward(0, z, x)
    forward(1, z, x)
    for offset in range(1, nx):
        piece = (x + offset) % nx
        arrived_q(z, piece)
        forward(0, z, piece)
        forward(1, z, piece)

    loads[5].wait()
    weight = wraw[...]
    wdup[...] = jnp.concatenate([weight, weight], axis=1)
    loads[1].wait()
    loads[2].wait()

    ref_index = lax.broadcasted_iota(jnp.int32, (1, refs), 1) + z * refs
    bias = jnp.where(ref_index < len_ref[0], jnp.float32(0.0), jnp.float32(-1e30))
    lane = lax.broadcasted_iota(jnp.int32, (block, HD), 1)

    def joined(ref, index, h):
        span = pl.ds(h * HD, HD)
        parts = [ref[index + (p, slice(None), span)].astype(F32) for p in range(nx)]
        return (jnp.concatenate(parts, axis=0) if nx > 1 else parts[0]).astype(BF16)

    def attend(b, h, key_rows, value_rows, bias_row):
        scores = dot_t(joined(qbuf, (b,), h), key_rows)
        if bias_row is not None:
            scores = scores + bias_row
        top = jnp.max(scores, axis=1, keepdims=True)
        weights = jnp.exp2((scores - top) * FACTOR).astype(BF16)
        ones = jnp.ones(value_rows.shape, BF16)
        summed = jnp.dot(
            weights, jnp.concatenate([value_rows, ones], axis=1), preferred_element_type=F32
        )
        return top, summed[:, :HD], summed[:, HD:]

    def ref_part(b):
        tops = jnp.zeros((block, HD), F32)
        totals = jnp.ones((block, HD), F32)
        for h in range(heads):
            span = pl.ds(h * HD, HD)
            top, summed, total = attend(b, h, rkey[:, span], rval[:, span], bias)
            oref[b, :, span] = summed
            tops = jnp.where(lane == h, top, tops)
            totals = jnp.where(lane == h, total, totals)
        mstat[b, pl.ds(0, block), :] = tops
        lstat[b, pl.ds(0, block), :] = totals

    def lse_copy(b, offset):
        to = (z + offset) % n
        return pltpu.make_async_remote_copy(
            src_ref=lse.at[z, b],
            dst_ref=lse.at[z, b],
            send_sem=s_send.at[offset, b],
            recv_sem=s_recv.at[z, b],
            device_id={"seq": to},
            device_id_type=MESH,
        )

    def self_part(b):
        tops = mstat[b, pl.ds(0, block), :]
        totals = lstat[b, pl.ds(0, block), :]
        for h in range(heads):
            span = pl.ds(h * HD, HD)
            top, summed, total = attend(b, h, kself[:, span], vself[:, span], None)
            oself[b, :, span] = summed
            tops = jnp.where(lane == heads + h, top, tops)
            totals = jnp.where(lane == heads + h, total, totals)
        tops = tops * FACTOR
        mstat[b, pl.ds(0, block), :] = tops
        lstat[b, pl.ds(0, block), :] = tops + jnp.log2(totals)
        for start in range(0, padded, HD):
            turned = lstat[b, pl.ds(start, HD), :].T
            lse[z, b, :, pl.ds(start, HD)] = turned[:lanes_used, :]
        for offset in range(1, n):
            lse_copy(b, offset).start()

    def receive_step(s):
        for side in range(2):
            b = z - s if side == 0 else z + s

            @pl.when((b >= 0) if side == 0 else (b < n))
            def _():
                for piece in range(nx):
                    arrived_q(b, piece)
                    forward(side, b, piece)

    def each_side(s, work):
        def one(side, carry):
            b = z + s * (2 * side - 1)

            @pl.when((b >= 0) & (b < n))
            def _():
                work(b)

            return carry

        lax.fori_loop(0, 2, one, 0)

    def block_of(j):
        return z + ((j + 1) // 2) * (1 - 2 * (j % 2))

    def visit(j, carry):
        b = block_of(j)

        @pl.when((j % 2 == 1))
        def _():
            receive_step((j + 1) // 2)

        @pl.when((b >= 0) & (b < n))
        def _():
            ref_part(b)

        @pl.when(j == min(2, 2 * n - 2))
        def _():
            loads[3].wait()
            loads[4].wait()
            for offset in range(1, nx):
                for kind in (1, 2):
                    other = (x + offset) % nx
                    target = (kbuf, vbuf)[kind - 1].at[other]
                    pltpu.make_async_remote_copy(
                        src_ref=target,
                        dst_ref=target,
                        send_sem=x_send.at[kind, offset],
                        recv_sem=kv_recv.at[kind - 1, other],
                        device_id={"blk": other},
                        device_id_type=MESH,
                    ).wait_recv()
            for h in range(heads):
                span = pl.ds(h * HD, HD)
                kself[:, span] = joined(kbuf, (), h)
                vself[:, span] = joined(vbuf, (), h)

        low = jnp.where(j == 2, 0, j) if n > 1 else j
        high = jnp.where(j < min(2, 2 * n - 2), low, j + 1)

        def late(i, inner):
            d = block_of(i)

            @pl.when((d >= 0) & (d < n))
            def _():
                self_part(d)

            return inner

        lax.fori_loop(low, high, late, 0)
        return carry

    lax.fori_loop(0, 2 * n - 1, visit, 0)

    gain = jnp.where(c == 0, guide_ref[0], 1.0 - guide_ref[0])
    half_lane = lax.broadcasted_iota(jnp.int32, (half, HD), 1)

    def slab_copy(index):
        return pltpu.make_async_remote_copy(
            src_ref=slab.at[index],
            dst_ref=landed.at[me],
            send_sem=v_send.at[index],
            recv_sem=v_recv.at[me],
            device_id=coords(index),
            device_id_type=MESH,
        )

    def project(i, carry):
        b = (i + 1) % n
        for offset in range(1, n):
            source = (z + offset) % n
            pltpu.make_async_remote_copy(
                src_ref=lse.at[source, b],
                dst_ref=lse.at[source, b],
                send_sem=s_send.at[offset, b],
                recv_sem=s_recv.at[source, b],
                device_id={"seq": source},
                device_id_type=MESH,
            ).wait_recv()
        for start in range(0, padded, HD):
            span = pl.ds(start, HD)
            parts = [lse[source, b, :, span] for source in range(n)]
            top = functools.reduce(jnp.maximum, parts)
            total = sum(jnp.exp2(part - top) for part in parts)
            whole = top + jnp.log2(total)
            pad = jnp.zeros((HD - lanes_used, HD), F32)
            lstat[b, span, :] = jnp.concatenate([whole, pad], axis=0).T
        share = jnp.exp2(mstat[b, pl.ds(0, block), :] - lstat[b, pl.ds(0, block), :])
        for h in range(heads):
            span = pl.ds(h * HD, HD)
            mixed = (
                share[:, h : h + 1] * oref[b, :, span]
                + share[:, heads + h : heads + h + 1] * oself[b, :, span]
            )
            att[:, span] = mixed.astype(BF16)
        vtmp[...] = gain * jnp.dot(att[...], wdup[...], preferred_element_type=F32)
        for other in range(nx):
            for branch in range(nc):
                first = other * rows + branch * 2 * half
                even = vtmp[pl.ds(first, half, stride=2), :]
                odd = vtmp[pl.ds(first + 1, half, stride=2), :]
                value = jnp.where(half_lane < HD // 2, even, odd)
                index = (b * nx + other) * nc + branch
                slab[index, pl.ds(0, half), :] = value

                @pl.when(index != me)
                def _():
                    slab_copy(index).start()

                @pl.when(index == me)
                def _():
                    landed[index, pl.ds(0, half), :] = value

        return carry

    lax.fori_loop(0, n, project, 0)

    for kind in range(3):
        for offset in range(1, nx):
            x_copy(offset, kind).wait_send()

    def sent(b, carry):
        for piece in range(nx):

            @pl.when((z < n - 1) & (b <= z))
            def _():
                z_copy(0, b, piece).wait_send()

            @pl.when((z > 0) & (b >= z))
            def _():
                z_copy(1, b, piece).wait_send()

        for offset in range(1, n):
            lse_copy(b, offset).wait_send()
        return carry

    lax.fori_loop(0, n, sent, 0)

    def collect(offset, carry):
        source = (me + offset) % members
        pltpu.make_async_remote_copy(
            src_ref=slab.at[source],
            dst_ref=landed.at[source],
            send_sem=v_send.at[source],
            recv_sem=v_recv.at[source],
            device_id=coords(source),
            device_id_type=MESH,
        ).wait()
        return carry

    lax.fori_loop(1, members, collect, 0)

    guided = jnp.sum(landed[:, pl.ds(0, half), :], axis=0)
    now = jnp.full((half, HD), step_ref[0], jnp.int32)
    sig_now = sigma_of(now.astype(F32))
    sig_next = sigma_of((now + 1).astype(F32))
    latent = latent_ref[...]
    next_ref[...] = latent + (sig_next - sig_now) * guided
    denoised_ref[...] = latent - sig_now * guided


def on_device(
    n,
    nx,
    nc,
    queries,
    keys,
    values,
    ref_keys,
    ref_values,
    ref_len,
    step_index,
    guide,
    latent,
    w_out,
):
    rows, wide = queries.shape[1:]
    refs = ref_keys.shape[1]
    width = wide // nx
    heads = width // HD
    block = nx * rows
    padded = round_up(block, HD)
    lanes_used = round_up(2 * heads, 8)
    members = n * nx * nc
    half = latent.shape[0]
    out = jax.ShapeDtypeStruct(latent.shape, F32)
    smem = pl.BlockSpec(memory_space=pltpu.SMEM)
    vmem = pl.BlockSpec(memory_space=pltpu.VMEM)
    anywhere = pl.BlockSpec(memory_space=pl.ANY)
    dma = pltpu.SemaphoreType.DMA
    flops = 4 * n * block * heads * HD * (refs + block)
    return pl.pallas_call(
        functools.partial(step_kernel, n, nx, nc),
        out_shape=(out, out),
        in_specs=[smem] * 3 + [anywhere] * 6 + [vmem],
        out_specs=(vmem, vmem),
        scratch_shapes=[
            pltpu.VMEM((n, nx, rows, width), BF16),
            pltpu.VMEM((nx, rows, width), BF16),
            pltpu.VMEM((nx, rows, width), BF16),
            pltpu.VMEM((refs, width), BF16),
            pltpu.VMEM((refs, width), BF16),
            pltpu.VMEM((width, w_out.shape[1]), BF16),
            pltpu.VMEM((width, 2 * w_out.shape[1]), BF16),
            pltpu.VMEM((block, width), BF16),
            pltpu.VMEM((block, width), BF16),
            pltpu.VMEM((n, block, width), F32),
            pltpu.VMEM((n, block, width), F32),
            pltpu.VMEM((n, padded, HD), F32),
            pltpu.VMEM((n, padded, HD), F32),
            pltpu.VMEM((n, n, lanes_used, padded), F32),
            pltpu.VMEM((block, width), BF16),
            pltpu.VMEM((block, HD), F32),
            pltpu.VMEM((members, round_up(half, 8), HD), F32),
            pltpu.VMEM((members, round_up(half, 8), HD), F32),
            dma((6,)),
            dma((3, nx)),
            dma((n, nx)),
            dma((2, nx)),
            dma((2, n, nx)),
            dma((n, n)),
            dma((n, n)),
            dma((members,)),
            dma((members,)),
        ],
        compiler_params=pltpu.CompilerParams(
            collective_id=0, has_side_effects=True, vmem_limit_bytes=58 * 2**20
        ),
        cost_estimate=pl.CostEstimate(
            flops=flops, bytes_accessed=4 * refs * width * 2, transcendentals=0
        ),
    )(ref_len, step_index, guide, queries, keys, values, ref_keys, ref_values, w_out, latent)


def solution(mesh):
    in_specs = (
        P(("groups", "cfg"), ("seq", "blk"), None),
        P(("groups", "cfg"), ("seq", "blk"), None),
        P(("groups", "cfg"), ("seq", "blk"), None),
        P(("groups", "cfg"), "seq", None),
        P(("groups", "cfg"), "seq", None),
        P(("groups", "cfg")),
        P("groups"),
        P("groups"),
        P(("groups", "seq", "blk", "cfg"), None),
        P(),
    )
    out_specs = (P(("groups", "seq", "blk", "cfg"), None), P(("groups", "seq", "blk", "cfg"), None))
    body = functools.partial(on_device, mesh.shape["seq"], mesh.shape["blk"], mesh.shape["cfg"])
    return jax.shard_map(
        body, mesh=mesh, in_specs=in_specs, out_specs=out_specs, check_vma=False
    )
```

time: 166 us -> 56.6 us (0.34)
  waiting for transfers between devices: 79.5 us -> 0 us
  Pallas kernels: 0 us -> 48.7 us
  blocking collectives: 30.2 us -> 0 us
  starting transfers between devices: 21.9 us -> 0 us
  local copies, waits for them, and re-layouts: 23.8 us -> 4.96 us
  matrix products: 4.52 us -> 0 us
  other arithmetic: 2.72 us -> 0 us
    all_to_all x5 -> x0, waiting for transfers between devices: 79.4 us -> none  [the longest x1 36.2 us: on_device(): lax.all_to_all(ref_values[0], 'seq', split_axis=1, concat_axis=0, tiled=T...]
    pallas_call x0 -> x1, Pallas kernels: none -> 48.7 us  [on_device(): pl.pallas_call(functools.partial(step_kernel, n, nx, nc), out_shape=(out,...]
    all_to_all x5 -> x0, starting transfers between devices: 21.9 us -> none  [the longest x1 6.32 us: on_device(): lax.all_to_all(query_local, 'seq', split_axis=1, concat_axis=0, tiled=True)]
    all_gather x2 -> x0, blocking collectives: 18.1 us -> none  [the longest x1 9.34 us: gather_keys(): lax.all_gather(key_rows, 'blk', axis=0, tiled=True)]
    all_to_all x11 -> x0, local copies, waits for them, and re-layouts: 17.6 us -> none  [the longest x2 8.04 us: on_device(): lax.all_to_all(ref_keys[0], 'seq', split_axis=1, concat_axis=0, tiled=True)]
    all_to_all x1 -> x0, blocking collectives: 12.1 us -> none  [on_device(): lax.all_to_all(attended, 'seq', split_axis=0, concat_axis=1, tiled=True)]
    dot_general x5 -> x0, matrix products: 4.52 us -> none  [the longest x1 1.75 us: reference_part(): jnp.einsum('rhp,phd->rhd', weights.astype(jnp.bfloat16), refvalue_all, pr...]
    reduce_sum x2 -> x0, other arithmetic: 2.09 us -> none  [the longest x1 1.33 us: reference_part(): return summed / jnp.sum(weights, axis=2)[..., None]]
  transfers between devices with their start and end apart: 6 -> 0, of which waited for: 5 -> 0; matrix products, arithmetic and copies ran while one was open for 6% -> 0% of each run, Pallas kernels for 0% -> 0%
where the time goes in v1:
time: 56.6 us; the launch traced here: 56.3 us
  Pallas kernels  48.7 us (86%)
  local copies, waits for them, and re-layouts  4.96 us (9%)
  between operations  2.58 us (5%)
    pallas_call x1, Pallas kernels, on_device(): pl.pallas_call(functools.partial(step_kernel, n, nx, nc), out_shape=(out,...  48.7 us
    unnamed x3, local copies, waits for them, and re-layouts  4.96 us

profile of v1, /device:TPU:0, one launch (start us, length us, event | category | flops | bytes accessed | tf_op | source)
XLA Modules:
  0.0 56.3 jit_solution(701282329250752446)
XLA Ops:
  2.6 2.4 %copy.12.w_ref = bf16[4096,64]{1,0:T(8,128)(2,1)} copy(bf16[4096,64]{0,1:T(8,128)(2,1)} %param.19) | data formatting | bytes 1048576 | tf_op args[9]
  4.9 48.7 %shard_map.113 = (f32[10,128]{1,0:T(8,128)}, f32[10,128]{1,0:T(8,128)}) custom-call(s32[1]{0:T(128)S(6)} %copy.15.len_ref, s32[1]{0:T(128)S(6)} %copy.16.step_ref, f32[1]{0:T(128)S(6)} %copy.17.guide_ref, bf16[1,40,4096]{2,1,0:T(8,128)(2,1)} %q_ref.1, bf16[1,40,4096]{2,1,0:T(8,128)(2,1)} %k_ref.1, bf16[1,40,4096]{2,1,0:T(8,128)(2,1)} %v_ref.1, ...), custom_call_target="tpu_custom_call" | custom-call | flops 880803840 | bytes 4194304 | tf_op jit(solution)/shard_map/pallas_call | solution.py:451
  53.7 1.3 %copy.18 = f32[10,128]{1,0:T(8,128)} copy(f32[10,128]{1,0:T(8,128)} %get-tuple-element.4) | data formatting | bytes 10240
  55.0 1.3 %copy.19 = f32[10,128]{1,0:T(8,128)} copy(f32[10,128]{1,0:T(8,128)} %get-tuple-element.5) | data formatting | bytes 10240

commit v2 on v1

v2 whole, which is shorter than its diff:
```python
import functools
import math

import jax
import jax.numpy as jnp
from jax import lax
from jax.experimental import pallas as pl
from jax.experimental.pallas import tpu as pltpu
from jax.sharding import PartitionSpec as P

HD = 128
STEPS = 50
FACTOR = HD ** (-0.5) * math.log2(math.e)
MESH = pl.DeviceIdType.MESH
BF16 = jnp.bfloat16
F32 = jnp.float32


def round_up(value, unit):
    return (value + unit - 1) // unit * unit


def sigma_of(frac_index):
    frac = 1.0 - frac_index / STEPS
    return 5.0 * frac / (1.0 + 4.0 * frac)


def dot_t(a, b):
    return lax.dot_general(a, b, (((1,), (1,)), ((), ())), preferred_element_type=F32)


def step_kernel(
    n,
    nx,
    nc,
    chunks,
    len_ref,
    step_ref,
    guide_ref,
    q_ref,
    k_ref,
    v_ref,
    rk_ref,
    rv_ref,
    w_ref,
    delta_ref,
    qbuf,
    kbuf,
    vbuf,
    rkey,
    rval,
    wdup,
    kself,
    vself,
    oref,
    oself,
    mstat,
    lstat,
    lse,
    att,
    vtmp,
    slab,
    landed,
    local_sem,
    x_send,
    kv_send,
    q_recv,
    kv_recv,
    z_send,
    s_send,
    s_recv,
    v_send,
    v_recv,
):
    z = lax.axis_index("seq")
    x = lax.axis_index("blk")
    c = lax.axis_index("cfg")
    rows = q_ref.shape[1]
    width = qbuf.shape[3]
    heads = width // HD
    per = heads // chunks
    part = per * HD
    block = nx * rows
    padded = lse.shape[3]
    lanes_used = lse.shape[2]
    half = delta_ref.shape[1]
    refs = rkey.shape[0]
    outs = w_ref.shape[0]
    late = min(2, max(1, n - 2))

    def cols(index):
        return pl.ds(pl.multiple_of(index * width, HD), width)

    def chunk(ch):
        return pl.ds(pl.multiple_of(ch * part, HD), part)

    loads = [
        pltpu.make_async_copy(q_ref.at[0, :, cols(x)], qbuf.at[z, x], local_sem.at[0]),
        pltpu.make_async_copy(rk_ref.at[0, :, cols(x)], rkey, local_sem.at[1]),
        pltpu.make_async_copy(rv_ref.at[0, :, cols(x)], rval, local_sem.at[2]),
        pltpu.make_async_copy(k_ref.at[0, :, cols(x)], kbuf.at[x], local_sem.at[3]),
        pltpu.make_async_copy(v_ref.at[0, :, cols(x)], vbuf.at[x], local_sem.at[4]),
        pltpu.make_async_copy(w_ref.at[:, cols(x)], wdup.at[pl.ds(0, outs)], local_sem.at[5]),
        pltpu.make_async_copy(w_ref.at[:, cols(x)], wdup.at[pl.ds(outs, outs)], local_sem.at[6]),
    ]
    for load in loads:
        load.start()

    members = n * nx * nc
    me = (z * nx + x) * nc + c

    def coords(index):
        return {"seq": index // (nx * nc), "blk": (index // nc) % nx, "cfg": index % nc}

    barrier = pltpu.get_barrier_semaphore()

    def greet(offset, carry):
        pl.semaphore_signal(
            barrier, inc=1, device_id=coords((me + offset) % members), device_id_type=MESH
        )
        return carry

    lax.fori_loop(1, members, greet, 0)
    pl.semaphore_wait(barrier, members - 1)

    def xq_copy(offset, ch):
        to = (x + offset) % nx
        span = pl.ds(pl.multiple_of(to * width + ch * part, HD), part)
        return pltpu.make_async_remote_copy(
            src_ref=q_ref.at[0, :, span],
            dst_ref=qbuf.at[z, x, :, chunk(ch)],
            send_sem=x_send.at[offset, ch],
            recv_sem=q_recv.at[z, x, ch],
            device_id={"blk": to},
            device_id_type=MESH,
        )

    def xkv_copy(offset, kind):
        to = (x + offset) % nx
        return pltpu.make_async_remote_copy(
            src_ref=(k_ref, v_ref)[kind].at[0, :, cols(to)],
            dst_ref=(kbuf, vbuf)[kind].at[x],
            send_sem=kv_send.at[kind, offset],
            recv_sem=kv_recv.at[kind, x],
            device_id={"blk": to},
            device_id_type=MESH,
        )

    def z_copy(side, b, piece, ch):
        ref = qbuf.at[b, piece, :, chunk(ch)]
        return pltpu.make_async_remote_copy(
            src_ref=ref,
            dst_ref=ref,
            send_sem=z_send.at[side, b, piece, ch],
            recv_sem=q_recv.at[b, piece, ch],
            device_id={"seq": z + 1 - 2 * side},
            device_id_type=MESH,
        )

    def forward(side, b, piece, ch):
        @pl.when((z < n - 1) if side == 0 else (z > 0))
        def _():
            z_copy(side, b, piece, ch).start()

    def arrived_q(b, piece, ch):
        ref = qbuf.at[b, piece, :, chunk(ch)]
        pltpu.make_async_remote_copy(
            src_ref=ref,
            dst_ref=ref,
            send_sem=z_send.at[0, b, piece, ch],
            recv_sem=q_recv.at[b, piece, ch],
            device_id={"blk": (x + 1) % nx},
            device_id_type=MESH,
        ).wait_recv()

    for ch in range(chunks):
        for offset in range(1, nx):
            xq_copy(offset, ch).start()
    loads[0].wait()
    for ch in range(chunks):
        forward(0, z, x, ch)
        forward(1, z, x, ch)
    for ch in range(chunks):
        for offset in range(1, nx):
            piece = (x + offset) % nx
            arrived_q(z, piece, ch)
            forward(0, z, piece, ch)
            forward(1, z, piece, ch)
    for kind in range(2):
        for offset in range(1, nx):
            xkv_copy(offset, kind).start()
    for load in loads[1:3] + loads[5:]:
        load.wait()

    ref_index = lax.broadcasted_iota(jnp.int32, (1, refs), 1) + z * refs
    bias = jnp.where(ref_index < len_ref[0], jnp.float32(0.0), jnp.float32(-1e30))
    lane = lax.broadcasted_iota(jnp.int32, (block, HD), 1)

    def joined(ref, index, span):
        parts = [ref[index + (p, slice(None), span)].astype(F32) for p in range(nx)]
        return (jnp.concatenate(parts, axis=0) if nx > 1 else parts[0]).astype(BF16)

    def attend(b, ch, with_ref, with_self):
        tops = mstat[b, pl.ds(0, block), :]
        totals = lstat[b, pl.ds(0, block), :]
        spans = [pl.ds(pl.multiple_of(ch * part + h * HD, HD), HD) for h in range(per)]
        kinds = ([0] if with_ref else []) + ([1] if with_self else [])
        tasks = [(h, kind) for h in range(per) for kind in kinds]

        def scores_of(task):
            h, kind = task
            if kind == 0 or not with_ref:
                queries[h] = joined(qbuf, (b,), spans[h])
            if kind == 0:
                return dot_t(queries[h], rkey[:, spans[h]]) + bias
            return dot_t(queries[h], kself[:, spans[h]])

        queries = {}
        pending = [scores_of(task) for task in tasks[:2]]
        for place, (h, kind) in enumerate(tasks):
            if place + 2 < len(tasks):
                pending.append(scores_of(tasks[place + 2]))
            scores = pending[place]
            top = jnp.max(scores, axis=1, keepdims=True)
            weights = jnp.exp2((scores - top) * FACTOR).astype(BF16)
            value_rows = (rval, vself)[kind][:, spans[h]]
            ones = jnp.ones(value_rows.shape, BF16)
            summed = jnp.dot(
                weights, jnp.concatenate([value_rows, ones], axis=1), preferred_element_type=F32
            )
            (oref, oself)[kind][b, :, spans[h]] = summed[:, :HD]
            here = lane == ch * per + h + kind * heads
            tops = jnp.where(here, top, tops)
            totals = jnp.where(here, summed[:, HD:], totals)
        mstat[b, pl.ds(0, block), :] = tops
        lstat[b, pl.ds(0, block), :] = totals

    def lse_copy(b, offset):
        to = (z + offset) % n
        return pltpu.make_async_remote_copy(
            src_ref=lse.at[z, b],
            dst_ref=lse.at[z, b],
            send_sem=s_send.at[offset, b],
            recv_sem=s_recv.at[z, b],
            device_id={"seq": to},
            device_id_type=MESH,
        )

    def finish(b):
        tops = mstat[b, pl.ds(0, block), :] * FACTOR
        mstat[b, pl.ds(0, block), :] = tops
        lstat[b, pl.ds(0, block), :] = tops + jnp.log2(lstat[b, pl.ds(0, block), :])
        for start in range(0, padded, HD):
            turned = lstat[b, pl.ds(start, HD), :].T
            lse[z, b, :, pl.ds(start, HD)] = turned[:lanes_used, :]
        for offset in range(1, n):
            lse_copy(b, offset).start()

    gain = jnp.where(c == 0, guide_ref[0], 1.0 - guide_ref[0])
    half_lane = lax.broadcasted_iota(jnp.int32, (half, HD), 1)

    def slab_copy(index):
        return pltpu.make_async_remote_copy(
            src_ref=slab.at[index],
            dst_ref=landed.at[me],
            send_sem=v_send.at[index],
            recv_sem=v_recv.at[me],
            device_id=coords(index),
            device_id_type=MESH,
        )

    def project(b):
        for offset in range(1, n):
            source = (z + offset) % n
            pltpu.make_async_remote_copy(
                src_ref=lse.at[source, b],
                dst_ref=lse.at[source, b],
                send_sem=s_send.at[offset, b],
                recv_sem=s_recv.at[source, b],
                device_id={"seq": source},
                device_id_type=MESH,
            ).wait_recv()
        for start in range(0, padded, HD):
            span = pl.ds(start, HD)
            parts = [lse[source, b, :, span] for source in range(n)]
            top = functools.reduce(jnp.maximum, parts)
            total = sum(jnp.exp2(part - top) for part in parts)
            whole = top + jnp.log2(total)
            pad = jnp.zeros((HD - lanes_used, HD), F32)
            lstat[b, span, :] = jnp.concatenate([whole, pad], axis=0).T
        share = jnp.exp2(mstat[b, pl.ds(0, block), :] - lstat[b, pl.ds(0, block), :])
        for h in range(heads):
            span = pl.ds(h * HD, HD)
            mixed = (
                share[:, h : h + 1] * oref[b, :, span]
                + share[:, heads + h : heads + h + 1] * oself[b, :, span]
            )
            att[:, span] = mixed.astype(BF16)
        vtmp[...] = gain * dot_t(att[...], wdup[...])
        for other in range(nx):
            for branch in range(nc):
                first = other * rows + branch * 2 * half
                even = vtmp[pl.ds(first, half, stride=2), :]
                odd = vtmp[pl.ds(first + 1, half, stride=2), :]
                value = jnp.where(half_lane < outs, even, odd)
                index = (b * nx + other) * nc + branch
                slab[index, pl.ds(0, half), :] = value

                @pl.when(index != me)
                def _():
                    slab_copy(index).start()

                @pl.when(index == me)
                def _():
                    landed[index, pl.ds(0, half), :] = value

    def block_of(i):
        return z + ((i + 1) // 2) * (1 - 2 * (i % 2))

    def each_block(low, high, work):
        def one(i, carry):
            b = block_of(i)

            @pl.when((b >= 0) & (b < n))
            def _():
                work(b)

            return carry

        lax.fori_loop(low, high, one, 0)

    def clear(b, carry):
        mstat[b] = jnp.zeros((padded, HD), F32)
        lstat[b] = jnp.ones((padded, HD), F32)
        return carry

    lax.fori_loop(0, n, clear, 0)

    def own_chunk(ch, carry):
        attend(z, ch, True, False)
        return carry

    lax.fori_loop(0, chunks, own_chunk, 0)

    def step(s, carry):
        if n > 2:

            @pl.when(s == n - 1)
            def _():
                def middle(b, inner):
                    project(b)
                    return inner

                lax.fori_loop(1, n - 1, middle, 0)

        @pl.when(s == late)
        def _():
            loads[3].wait()
            loads[4].wait()
            for offset in range(1, nx):
                for kind in range(2):
                    other = (x + offset) % nx
                    target = (kbuf, vbuf)[kind].at[other]
                    pltpu.make_async_remote_copy(
                        src_ref=target,
                        dst_ref=target,
                        send_sem=kv_send.at[kind, offset],
                        recv_sem=kv_recv.at[kind, other],
                        device_id={"blk": other},
                        device_id_type=MESH,
                    ).wait_recv()
            for h in range(heads):
                span = pl.ds(h * HD, HD)
                kself[:, span] = joined(kbuf, (), span)
                vself[:, span] = joined(vbuf, (), span)

        def each_chunk(ch, inner):
            for side in range(2):
                b = z - s if side == 0 else z + s

                @pl.when((b >= 0) if side == 0 else (b < n))
                def _():
                    for offset in range(nx):
                        piece = (x + offset) % nx
                        arrived_q(b, piece, ch)
                        forward(side, b, piece, ch)

            @pl.when(s < late)
            def _():
                each_block(2 * s - 1, 2 * s + 1, lambda b: attend(b, ch, True, False))

            @pl.when(s >= late)
            def _():
                each_block(2 * s - 1, 2 * s + 1, lambda b: attend(b, ch, True, True))

            @pl.when(s == late)
            def _():
                each_block(0, 2 * late - 1, lambda b: attend(b, ch, False, True))

            return inner

        lax.fori_loop(0, chunks, each_chunk, 0)

        @pl.when(s >= late)
        def _():
            each_block(jnp.where(s == late, 0, 2 * s - 1), 2 * s + 1, finish)

        return carry

    lax.fori_loop(1, n, step, 0)

    def ends(i, carry):
        project(i * (n - 1))
        return carry

    lax.fori_loop(0, 2, ends, 0)

    for offset in range(1, nx):
        for ch in range(chunks):
            xq_copy(offset, ch).wait_send()
        for kind in range(2):
            xkv_copy(offset, kind).wait_send()

    def sent(b, carry):
        for piece in range(nx):
            for ch in range(chunks):

                @pl.when((z < n - 1) & (b <= z))
                def _():
                    z_copy(0, b, piece, ch).wait_send()

                @pl.when((z > 0) & (b >= z))
                def _():
                    z_copy(1, b, piece, ch).wait_send()

        for offset in range(1, n):
            lse_copy(b, offset).wait_send()
        return carry

    lax.fori_loop(0, n, sent, 0)

    def collect(offset, carry):
        source = (me + offset) % members
        pltpu.make_async_remote_copy(
            src_ref=slab.at[source],
            dst_ref=landed.at[source],
            send_sem=v_send.at[source],
            recv_sem=v_recv.at[source],
            device_id=coords(source),
            device_id_type=MESH,
        ).wait()
        return carry

    lax.fori_loop(1, members, collect, 0)

    guided = jnp.sum(landed[:, pl.ds(0, half), :], axis=0)
    now = jnp.full((half, HD), step_ref[0], jnp.int32)
    sig_now = sigma_of(now.astype(F32))
    sig_next = sigma_of((now + 1).astype(F32))
    delta_ref[0] = (sig_next - sig_now) * guided
    delta_ref[1] = sig_now * guided


def on_device(
    n,
    nx,
    nc,
    queries,
    keys,
    values,
    ref_keys,
    ref_values,
    ref_len,
    step_index,
    guide,
    latent,
    w_out,
):
    rows, wide = queries.shape[1:]
    refs = ref_keys.shape[1]
    width = wide // nx
    heads = width // HD
    block = nx * rows
    padded = round_up(block, HD)
    lanes_used = round_up(2 * heads, 8)
    members = n * nx * nc
    half = latent.shape[0]
    chunks = 4 if heads % 4 == 0 and heads > 4 else 1
    smem = pl.BlockSpec(memory_space=pltpu.SMEM)
    vmem = pl.BlockSpec(memory_space=pltpu.VMEM)
    anywhere = pl.BlockSpec(memory_space=pl.ANY)
    dma = pltpu.SemaphoreType.DMA
    flops = 4 * n * block * heads * HD * (refs + block)
    delta = pl.pallas_call(
        functools.partial(step_kernel, n, nx, nc, chunks),
        out_shape=jax.ShapeDtypeStruct((2,) + latent.shape, F32),
        in_specs=[smem] * 3 + [anywhere] * 6,
        out_specs=vmem,
        scratch_shapes=[
            pltpu.VMEM((n, nx, rows, width), BF16),
            pltpu.VMEM((nx, rows, width), BF16),
            pltpu.VMEM((nx, rows, width), BF16),
            pltpu.VMEM((refs, width), BF16),
            pltpu.VMEM((refs, width), BF16),
            pltpu.VMEM((2 * w_out.shape[1], width), BF16),
            pltpu.VMEM((block, width), BF16),
            pltpu.VMEM((block, width), BF16),
            pltpu.VMEM((n, block, width), F32),
            pltpu.VMEM((n, block, width), F32),
            pltpu.VMEM((n, padded, HD), F32),
            pltpu.VMEM((n, padded, HD), F32),
            pltpu.VMEM((n, n, lanes_used, padded), F32),
            pltpu.VMEM((block, width), BF16),
            pltpu.VMEM((block, HD), F32),
            pltpu.VMEM((members, round_up(half, 8), HD), F32),
            pltpu.VMEM((members, round_up(half, 8), HD), F32),
            dma((7,)),
            dma((nx, chunks)),
            dma((2, nx)),
            dma((n, nx, chunks)),
            dma((2, nx)),
            dma((2, n, nx, chunks)),
            dma((n, n)),
            dma((n, n)),
            dma((members,)),
            dma((members,)),
        ],
        compiler_params=pltpu.CompilerParams(
            collective_id=0, has_side_effects=True, vmem_limit_bytes=58 * 2**20
        ),
        cost_estimate=pl.CostEstimate(
            flops=flops, bytes_accessed=4 * refs * width * 2, transcendentals=0
        ),
    )(ref_len, step_index, guide, queries, keys, values, ref_keys, ref_values, w_out.T)
    return latent + delta[0], latent - delta[1]


def solution(mesh):
    in_specs = (
        P(("groups", "cfg"), ("seq", "blk"), None),
        P(("groups", "cfg"), ("seq", "blk"), None),
        P(("groups", "cfg"), ("seq", "blk"), None),
        P(("groups", "cfg"), "seq", None),
        P(("groups", "cfg"), "seq", None),
        P(("groups", "cfg")),
        P("groups"),
        P("groups"),
        P(("groups", "seq", "blk", "cfg"), None),
        P(),
    )
    out_specs = (P(("groups", "seq", "blk", "cfg"), None), P(("groups", "seq", "blk", "cfg"), None))
    body = functools.partial(on_device, mesh.shape["seq"], mesh.shape["blk"], mesh.shape["cfg"])
    return jax.shard_map(
        body, mesh=mesh, in_specs=in_specs, out_specs=out_specs, check_vma=False
    )
```

time: 56.6 us -> 50.7 us (0.90)
  local copies, waits for them, and re-layouts: 4.96 us -> 0.01 us
  Pallas kernels: 48.7 us -> 46.6 us
  other arithmetic: 0 us -> 1.32 us
    unnamed x3 -> x2, local copies, waits for them, and re-layouts: 4.96 us -> 0.01 us
    pallas_call x1, Pallas kernels: 48.7 us -> 46.6 us  [on_device(): pl.pallas_call(functools.partial(step_kernel, n, nx, nc, chunks), out_sha...]
    sub x0 -> x1, other arithmetic: none -> 1.32 us  [on_device(): return (latent + delta[0], latent - delta[1])]
where the time goes in v2:
time: 50.7 us; the launch traced here: 50.5 us
  Pallas kernels  46.6 us (92%)
  between operations  2.59 us (5%)
  other arithmetic  1.32 us (3%)
    pallas_call x1, Pallas kernels, on_device(): pl.pallas_call(functools.partial(step_kernel, n, nx, nc, chunks), out_sha...  46.6 us
    sub x1, other arithmetic, on_device(): return (latent + delta[0], latent - delta[1])  1.32 us

profile of v2, /device:TPU:0, one launch (start us, length us, event | category | flops | bytes accessed | tf_op | source)
XLA Modules:
  0.0 50.5 jit_solution(15015343260822633403)
XLA Ops:
  2.6 0.0 copy-start
  2.6 46.6 %shard_map.113 = f32[2,10,128]{2,1,0:T(8,128)} custom-call(s32[1]{0:T(128)S(6)} %copy.12.len_ref, s32[1]{0:T(128)S(6)} %copy.13.step_ref, f32[1]{0:T(128)S(6)} %copy.14.guide_ref, bf16[1,40,4096]{2,1,0:T(8,128)(2,1)} %q_ref.1, bf16[1,40,4096]{2,1,0:T(8,128)(2,1)} %k_ref.1, bf16[1,40,4096]{2,1,0:T(8,128)(2,1)} %v_ref.1, bf16[1,256,4096]{2,1,0:T(8,128)(2,1)} %rk_ref.1, ...), custom_call_target="tpu_custom_call" | custom-call | flops 880803840 | bytes 4194304 | tf_op jit(solution)/shard_map/pallas_call | solution.py:494
  49.2 0.0 copy-done
  49.2 1.3 %bitcast_subtract_fusion = (f32[10,128]{1,0:T(8,128)}, f32[10,128]{1,0:T(8,128)}) fusion(f32[10,128]{1,0:T(8,128)S(1)} %copy-done, f32[2,10,128]{2,1,0:T(8,128)} %shard_map.113), kind=kLoop, calls=%fused_computation | loop fusion | flops 2560 | bytes 25600 | tf_op jit(solution)/shard_map/sub | solution.py:535
Async XLA Ops:
  2.6 46.6 %copy-start = (f32[10,128]{1,0:T(8,128)S(1)}, f32[10,128]{1,0:T(8,128)}, u32[]{:S(2)}) copy-start(f32[10,128]{1,0:T(8,128)} %param.18) | copy-start | bytes 15364

commit v3 on v2

--- a/solution.py
+++ b/solution.py
@@ -13,6 +13,7 @@
 FACTOR = HD ** (-0.5) * math.log2(math.e)
 MESH = pl.DeviceIdType.MESH
 BF16 = jnp.bfloat16
+ONES = 16
 F32 = jnp.float32
 
 
@@ -51,13 +52,16 @@
     rval,
     wdup,
     kself,
-    vself,
+    mask,
+    rturn,
+    sturn,
     oref,
     oself,
     mstat,
     lstat,
     lse,
     att,
+    vwide,
     vtmp,
     slab,
     landed,
@@ -81,8 +85,7 @@
     per = heads // chunks
     part = per * HD
     block = nx * rows
-    padded = lse.shape[3]
-    lanes_used = lse.shape[2]
+    padded = vtmp.shape[0]
     half = delta_ref.shape[1]
     refs = rkey.shape[0]
     outs = w_ref.shape[0]
@@ -121,6 +124,10 @@
         return carry
 
     lax.fori_loop(1, members, greet, 0)
+    ref_index = lax.broadcasted_iota(jnp.int32, (refs, block), 0) + z * refs
+    mask[...] = jnp.where(ref_index < len_ref[0], jnp.float32(0.0), jnp.float32(-1e30))
+    rturn[:, pl.ds(HD, ONES), :] = jnp.ones((heads, ONES, refs), BF16)
+    sturn[:, pl.ds(HD, ONES), :] = jnp.ones((heads, ONES, block), BF16)
     pl.semaphore_wait(barrier, members - 1)
 
     def xq_copy(offset, ch):
@@ -180,6 +187,10 @@
     for ch in range(chunks):
         forward(0, z, x, ch)
         forward(1, z, x, ch)
+    for load in loads[1:3] + loads[5:]:
+        load.wait()
+    for h in range(heads):
+        rturn[h, pl.ds(0, HD), :] = rval[:, pl.ds(h * HD, HD)].astype(F32).T.astype(BF16)
     for ch in range(chunks):
         for offset in range(1, nx):
             piece = (x + offset) % nx
@@ -189,51 +200,46 @@
     for kind in range(2):
         for offset in range(1, nx):
             xkv_copy(offset, kind).start()
-    for load in loads[1:3] + loads[5:]:
-        load.wait()
-
-    ref_index = lax.broadcasted_iota(jnp.int32, (1, refs), 1) + z * refs
-    bias = jnp.where(ref_index < len_ref[0], jnp.float32(0.0), jnp.float32(-1e30))
-    lane = lax.broadcasted_iota(jnp.int32, (block, HD), 1)
 
     def joined(ref, index, span):
         parts = [ref[index + (p, slice(None), span)].astype(F32) for p in range(nx)]
-        return (jnp.concatenate(parts, axis=0) if nx > 1 else parts[0]).astype(BF16)
+        return jnp.concatenate(parts, axis=0) if nx > 1 else parts[0]
 
     def attend(b, ch, with_ref, with_self):
-        tops = mstat[b, pl.ds(0, block), :]
-        totals = lstat[b, pl.ds(0, block), :]
         spans = [pl.ds(pl.multiple_of(ch * part + h * HD, HD), HD) for h in range(per)]
         kinds = ([0] if with_ref else []) + ([1] if with_self else [])
-        tasks = [(h, kind) for h in range(per) for kind in kinds]
-
-        def scores_of(task):
-            h, kind = task
-            if kind == 0 or not with_ref:
-                queries[h] = joined(qbuf, (b,), spans[h])
-            if kind == 0:
-                return dot_t(queries[h], rkey[:, spans[h]]) + bias
-            return dot_t(queries[h], kself[:, spans[h]])
-
-        queries = {}
-        pending = [scores_of(task) for task in tasks[:2]]
-        for place, (h, kind) in enumerate(tasks):
-            if place + 2 < len(tasks):
-                pending.append(scores_of(tasks[place + 2]))
-            scores = pending[place]
-            top = jnp.max(scores, axis=1, keepdims=True)
-            weights = jnp.exp2((scores - top) * FACTOR).astype(BF16)
-            value_rows = (rval, vself)[kind][:, spans[h]]
-            ones = jnp.ones(value_rows.shape, BF16)
-            summed = jnp.dot(
-                weights, jnp.concatenate([value_rows, ones], axis=1), preferred_element_type=F32
-            )
-            (oref, oself)[kind][b, :, spans[h]] = summed[:, :HD]
-            here = lane == ch * per + h + kind * heads
-            tops = jnp.where(here, top, tops)
-            totals = jnp.where(here, summed[:, HD:], totals)
-        mstat[b, pl.ds(0, block), :] = tops
-        lstat[b, pl.ds(0, block), :] = totals
+        group = min(2, per)
+
+        def scores_of(first):
+            found = []
+            for h in range(first, first + group):
+                query = joined(qbuf, (b,), spans[h]).astype(BF16)
+                for kind in kinds:
+                    scores = dot_t((rkey, kself)[kind][:, spans[h]], query)
+                    found.append((h, kind, scores + mask[...] if kind == 0 else scores))
+            return found
+
+        upcoming = scores_of(0)
+        for first in range(0, per, group):
+            current = upcoming
+            if first + group < per:
+                upcoming = scores_of(first + group)
+            tops = [jnp.max(scores, axis=0, keepdims=True) for _, _, scores in current]
+            weights = [
+                jnp.exp2((scores - top) * FACTOR).astype(BF16)
+                for (_, _, scores), top in zip(current, tops)
+            ]
+            sums = [
+                jnp.dot(
+                    (rturn, sturn)[kind][ch * per + h], weight, preferred_element_type=F32
+                )
+                for (h, kind, _), weight in zip(current, weights)
+            ]
+            for (h, kind, _), top, summed in zip(current, tops, sums):
+                (oref, oself)[kind][b, ch * per + h] = summed[:HD]
+                row = pl.ds(ch * per + h + kind * heads, 1)
+                mstat[b, row, :] = top
+                lstat[b, row, :] = summed[HD : HD + 1]
 
     def lse_copy(b, offset):
         to = (z + offset) % n
@@ -247,12 +253,7 @@
         )
 
     def finish(b):
-        tops = mstat[b, pl.ds(0, block), :] * FACTOR
-        mstat[b, pl.ds(0, block), :] = tops
-        lstat[b, pl.ds(0, block), :] = tops + jnp.log2(lstat[b, pl.ds(0, block), :])
-        for start in range(0, padded, HD):
-            turned = lstat[b, pl.ds(start, HD), :].T
-            lse[z, b, :, pl.ds(start, HD)] = turned[:lanes_used, :]
+        lse[z, b] = mstat[b] * FACTOR + jnp.log2(lstat[b])
         for offset in range(1, n):
             lse_copy(b, offset).start()
 
@@ -280,23 +281,21 @@
                 device_id={"seq": source},
                 device_id_type=MESH,
             ).wait_recv()
+        parts = [lse[source, b] for source in range(n)]
+        top = functools.reduce(jnp.maximum, parts)
+        total = sum(jnp.exp2(part - top) for part in parts)
+        share = jnp.exp2(mstat[b] * FACTOR - top - jnp.log2(total))
+        for h in range(heads):
+            mixed = (
+                share[h : h + 1] * oref[b, h] + share[heads + h : heads + h + 1] * oself[b, h]
+            )
+            att[pl.ds(h * HD, HD), :] = mixed.astype(BF16)
+        vwide[:, pl.ds(0, block)] = gain * jnp.dot(
+            wdup[...], att[...], preferred_element_type=F32
+        )
         for start in range(0, padded, HD):
             span = pl.ds(start, HD)
-            parts = [lse[source, b, :, span] for source in range(n)]
-            top = functools.reduce(jnp.maximum, parts)
-            total = sum(jnp.exp2(part - top) for part in parts)
-            whole = top + jnp.log2(total)
-            pad = jnp.zeros((HD - lanes_used, HD), F32)
-            lstat[b, span, :] = jnp.concatenate([whole, pad], axis=0).T
-        share = jnp.exp2(mstat[b, pl.ds(0, block), :] - lstat[b, pl.ds(0, block), :])
-        for h in range(heads):
-            span = pl.ds(h * HD, HD)
-            mixed = (
-                share[:, h : h + 1] * oref[b, :, span]
-                + share[:, heads + h : heads + h + 1] * oself[b, :, span]
-            )
-            att[:, span] = mixed.astype(BF16)
-        vtmp[...] = gain * dot_t(att[...], wdup[...])
+            vtmp[span, :] = vwide[:, span].T
         for other in range(nx):
             for branch in range(nc):
                 first = other * rows + branch * 2 * half
@@ -328,13 +327,6 @@
             return carry
 
         lax.fori_loop(low, high, one, 0)
-
-    def clear(b, carry):
-        mstat[b] = jnp.zeros((padded, HD), F32)
-        lstat[b] = jnp.ones((padded, HD), F32)
-        return carry
-
-    lax.fori_loop(0, n, clear, 0)
 
     def own_chunk(ch, carry):
         attend(z, ch, True, False)
@@ -371,8 +363,8 @@
                     ).wait_recv()
             for h in range(heads):
                 span = pl.ds(h * HD, HD)
-                kself[:, span] = joined(kbuf, (), span)
-                vself[:, span] = joined(vbuf, (), span)
+                kself[:, span] = joined(kbuf, (), span).astype(BF16)
+                sturn[h, pl.ds(0, HD), :] = joined(vbuf, (), span).T.astype(BF16)
 
         def each_chunk(ch, inner):
             for side in range(2):
@@ -482,7 +474,7 @@
     heads = width // HD
     block = nx * rows
     padded = round_up(block, HD)
-    lanes_used = round_up(2 * heads, 8)
+    stats = round_up(2 * heads, 8)
     members = n * nx * nc
     half = latent.shape[0]
     chunks = 4 if heads % 4 == 0 and heads > 4 else 1
@@ -504,14 +496,17 @@
             pltpu.VMEM((refs, width), BF16),
             pltpu.VMEM((2 * w_out.shape[1], width), BF16),
             pltpu.VMEM((block, width), BF16),
-            pltpu.VMEM((block, width), BF16),
-            pltpu.VMEM((n, block, width), F32),
-            pltpu.VMEM((n, block, width), F32),
-            pltpu.VMEM((n, padded, HD), F32),
-            pltpu.VMEM((n, padded, HD), F32),
-            pltpu.VMEM((n, n, lanes_used, padded), F32),
-            pltpu.VMEM((block, width), BF16),
-            pltpu.VMEM((block, HD), F32),
+            pltpu.VMEM((refs, block), F32),
+            pltpu.VMEM((heads, HD + ONES, refs), BF16),
+            pltpu.VMEM((heads, HD + ONES, block), BF16),
+            pltpu.VMEM((n, heads, HD, block), F32),
+            pltpu.VMEM((n, heads, HD, block), F32),
+            pltpu.VMEM((n, stats, block), F32),
+            pltpu.VMEM((n, stats, block), F32),
+            pltpu.VMEM((n, n, stats, block), F32),
+            pltpu.VMEM((width, block), BF16),
+            pltpu.VMEM((HD, padded), F32),
+            pltpu.VMEM((padded, HD), F32),
             pltpu.VMEM((members, round_up(half, 8), HD), F32),
             pltpu.VMEM((members, round_up(half, 8), HD), F32),
             dma((7,)),

time: 50.7 us -> 50 us (0.986)
  Pallas kernels: 46.6 us -> 45.9 us
    pallas_call x1, Pallas kernels: 46.6 us -> 45.9 us  [on_device(): pl.pallas_call(functools.partial(step_kernel, n, nx, nc, chunks), out_sha...]
where the time goes in v3:
time: 50 us; the launch traced here: 49.8 us
  Pallas kernels  45.9 us (92%)
  between operations  2.59 us (5%)
  other arithmetic  1.32 us (3%)
    pallas_call x1, Pallas kernels, on_device(): pl.pallas_call(functools.partial(step_kernel, n, nx, nc, chunks), out_sha...  45.9 us
    sub x1, other arithmetic, on_device(): return (latent + delta[0], latent - delta[1])  1.32 us

profile of v3, /device:TPU:0, one launch (start us, length us, event | category | flops | bytes accessed | tf_op | source)
XLA Modules:
  0.0 49.8 jit_solution(18168355606036946910)
XLA Ops:
  2.6 0.0 copy-start
  2.6 45.9 %shard_map.113 = f32[2,10,128]{2,1,0:T(8,128)} custom-call(s32[1]{0:T(128)S(6)} %copy.12.len_ref, s32[1]{0:T(128)S(6)} %copy.13.step_ref, f32[1]{0:T(128)S(6)} %copy.14.guide_ref, bf16[1,40,4096]{2,1,0:T(8,128)(2,1)} %q_ref.1, bf16[1,40,4096]{2,1,0:T(8,128)(2,1)} %k_ref.1, bf16[1,40,4096]{2,1,0:T(8,128)(2,1)} %v_ref.1, bf16[1,256,4096]{2,1,0:T(8,128)(2,1)} %rk_ref.1, ...), custom_call_target="tpu_custom_call" | custom-call | flops 880803840 | bytes 4194304 | tf_op jit(solution)/shard_map/pallas_call | solution.py:486
  48.5 0.0 copy-done
  48.5 1.3 %bitcast_subtract_fusion = (f32[10,128]{1,0:T(8,128)}, f32[10,128]{1,0:T(8,128)}) fusion(f32[10,128]{1,0:T(8,128)S(1)} %copy-done, f32[2,10,128]{2,1,0:T(8,128)} %shard_map.113), kind=kLoop, calls=%fused_computation | loop fusion | flops 2560 | bytes 25600 | tf_op jit(solution)/shard_map/sub | solution.py:530
Async XLA Ops:
  2.6 45.9 %copy-start = (f32[10,128]{1,0:T(8,128)S(1)}, f32[10,128]{1,0:T(8,128)}, u32[]{:S(2)}) copy-start(f32[10,128]{1,0:T(8,128)} %param.18) | copy-start | bytes 15364

commit v4 on v3

--- a/solution.py
+++ b/solution.py
@@ -89,7 +89,7 @@
     half = delta_ref.shape[1]
     refs = rkey.shape[0]
     outs = w_ref.shape[0]
-    late = min(2, max(1, n - 2))
+    late = min(2, n - 1)
 
     def cols(index):
         return pl.ds(pl.multiple_of(index * width, HD), width)
@@ -187,10 +187,6 @@
     for ch in range(chunks):
         forward(0, z, x, ch)
         forward(1, z, x, ch)
-    for load in loads[1:3] + loads[5:]:
-        load.wait()
-    for h in range(heads):
-        rturn[h, pl.ds(0, HD), :] = rval[:, pl.ds(h * HD, HD)].astype(F32).T.astype(BF16)
     for ch in range(chunks):
         for offset in range(1, nx):
             piece = (x + offset) % nx
@@ -328,25 +324,44 @@
 
         lax.fori_loop(low, high, one, 0)
 
-    def own_chunk(ch, carry):
+    def receive(s, ch):
+        for side in range(2):
+            b = z - s if side == 0 else z + s
+
+            @pl.when((b >= 0) if side == 0 else (b < n))
+            def _():
+                for offset in range(nx):
+                    piece = (x + offset) % nx
+                    arrived_q(b, piece, ch)
+                    forward(side, b, piece, ch)
+
+    def each_chunk(work):
+        def one(ch, carry):
+            work(ch)
+            return carry
+
+        lax.fori_loop(0, chunks, one, 0)
+
+    for load in loads[1:3] + loads[5:]:
+        load.wait()
+
+    def own_chunk(ch):
+        receive(1, ch)
+        for h in range(per):
+            span = pl.ds(pl.multiple_of(ch * part + h * HD, HD), HD)
+            turned = rval[:, span].astype(F32).T
+            rturn[ch * per + h, pl.ds(0, HD), :] = turned.astype(BF16)
         attend(z, ch, True, False)
-        return carry
-
-    lax.fori_loop(0, chunks, own_chunk, 0)
+
+    each_chunk(own_chunk)
+    if late > 1:
+        each_chunk(lambda ch: each_block(1, 3, lambda b: attend(b, ch, True, False)))
 
     def step(s, carry):
-        if n > 2:
-
-            @pl.when(s == n - 1)
-            def _():
-                def middle(b, inner):
-                    project(b)
-                    return inner
-
-                lax.fori_loop(1, n - 1, middle, 0)
-
         @pl.when(s == late)
         def _():
+            if late > 1:
+                each_chunk(lambda ch: receive(s, ch))
             loads[3].wait()
             loads[4].wait()
             for offset in range(1, nx):
@@ -366,40 +381,32 @@
                 kself[:, span] = joined(kbuf, (), span).astype(BF16)
                 sturn[h, pl.ds(0, HD), :] = joined(vbuf, (), span).T.astype(BF16)
 
-        def each_chunk(ch, inner):
-            for side in range(2):
-                b = z - s if side == 0 else z + s
-
-                @pl.when((b >= 0) if side == 0 else (b < n))
-                def _():
-                    for offset in range(nx):
-                        piece = (x + offset) % nx
-                        arrived_q(b, piece, ch)
-                        forward(side, b, piece, ch)
-
-            @pl.when(s < late)
+        def work(ch):
+            @pl.when(s > late)
             def _():
-                each_block(2 * s - 1, 2 * s + 1, lambda b: attend(b, ch, True, False))
-
-            @pl.when(s >= late)
-            def _():
-                each_block(2 * s - 1, 2 * s + 1, lambda b: attend(b, ch, True, True))
-
-            @pl.when(s == late)
-            def _():
-                each_block(0, 2 * late - 1, lambda b: attend(b, ch, False, True))
-
-            return inner
-
-        lax.fori_loop(0, chunks, each_chunk, 0)
-
-        @pl.when(s >= late)
+                receive(s, ch)
+
+            each_block(2 * s - 1, 2 * s + 1, lambda b: attend(b, ch, True, True))
+
+        each_chunk(work)
+        each_block(2 * s - 1, 2 * s + 1, finish)
+
+        @pl.when(s == late)
         def _():
-            each_block(jnp.where(s == late, 0, 2 * s - 1), 2 * s + 1, finish)
+            each_chunk(
+                lambda ch: each_block(0, 2 * late - 1, lambda b: attend(b, ch, False, True))
+            )
+            each_block(0, 2 * late - 1, finish)
 
         return carry
 
-    lax.fori_loop(1, n, step, 0)
+    lax.fori_loop(late, n, step, 0)
+
+    def middle(b, carry):
+        project(b)
+        return carry
+
+    lax.fori_loop(1, n - 1, middle, 0)
 
     def ends(i, carry):
         project(i * (n - 1))

time: 50 us -> 45.8 us (0.916)
  Pallas kernels: 45.9 us -> 41.7 us
    pallas_call x1, Pallas kernels: 45.9 us -> 41.7 us  [on_device(): pl.pallas_call(functools.partial(step_kernel, n, nx, nc, chunks), out_sha...]
where the time goes in v4:
time: 45.8 us; the launch traced here: 45.6 us
  Pallas kernels  41.7 us (91%)
  between operations  2.59 us (6%)
  other arithmetic  1.32 us (3%)
    pallas_call x1, Pallas kernels, on_device(): pl.pallas_call(functools.partial(step_kernel, n, nx, nc, chunks), out_sha...  41.7 us
    sub x1, other arithmetic, on_device(): return (latent + delta[0], latent - delta[1])  1.32 us

profile of v4, /device:TPU:0, one launch (start us, length us, event | category | flops | bytes accessed | tf_op | source)
XLA Modules:
  0.0 45.6 jit_solution(2227296149900734004)
XLA Ops:
  2.6 0.0 copy-start
  2.6 41.7 %shard_map.113 = f32[2,10,128]{2,1,0:T(8,128)} custom-call(s32[1]{0:T(128)S(6)} %copy.12.len_ref, s32[1]{0:T(128)S(6)} %copy.13.step_ref, f32[1]{0:T(128)S(6)} %copy.14.guide_ref, bf16[1,40,4096]{2,1,0:T(8,128)(2,1)} %q_ref.1, bf16[1,40,4096]{2,1,0:T(8,128)(2,1)} %k_ref.1, bf16[1,40,4096]{2,1,0:T(8,128)(2,1)} %v_ref.1, bf16[1,256,4096]{2,1,0:T(8,128)(2,1)} %rk_ref.1, ...), custom_call_target="tpu_custom_call" | custom-call | flops 880803840 | bytes 4194304 | tf_op jit(solution)/shard_map/pallas_call | solution.py:493
  44.3 0.0 copy-done
  44.3 1.3 %bitcast_subtract_fusion = (f32[10,128]{1,0:T(8,128)}, f32[10,128]{1,0:T(8,128)}) fusion(f32[10,128]{1,0:T(8,128)S(1)} %copy-done, f32[2,10,128]{2,1,0:T(8,128)} %shard_map.113), kind=kLoop, calls=%fused_computation | loop fusion | flops 2560 | bytes 25600 | tf_op jit(solution)/shard_map/sub | solution.py:537
Async XLA Ops:
  2.6 41.7 %copy-start = (f32[10,128]{1,0:T(8,128)S(1)}, f32[10,128]{1,0:T(8,128)}, u32[]{:S(2)}) copy-start(f32[10,128]{1,0:T(8,128)} %param.18) | copy-start | bytes 15364

commit v5 on v4

--- a/solution.py
+++ b/solution.py
@@ -355,13 +355,16 @@
 
     each_chunk(own_chunk)
     if late > 1:
-        each_chunk(lambda ch: each_block(1, 3, lambda b: attend(b, ch, True, False)))
+
+        def next_chunk(ch):
+            each_block(1, 3, lambda b: attend(b, ch, True, False))
+            receive(2, ch)
+
+        each_chunk(next_chunk)
 
     def step(s, carry):
         @pl.when(s == late)
         def _():
-            if late > 1:
-                each_chunk(lambda ch: receive(s, ch))
             loads[3].wait()
             loads[4].wait()
             for offset in range(1, nx):
@@ -409,7 +412,7 @@
     lax.fori_loop(1, n - 1, middle, 0)
 
     def ends(i, carry):
-        project(i * (n - 1))
+        project(jnp.where(2 * z < n, 1 - i, i) * (n - 1))
         return carry
 
     lax.fori_loop(0, 2, ends, 0)

time: 45.8 us -> 46.1 us (level)
  no operation moved by 1% of the time
where the time goes in v5:
time: 46.1 us; the launch traced here: 45.8 us
  Pallas kernels  41.9 us (91%)
  between operations  2.59 us (6%)
  other arithmetic  1.32 us (3%)
    pallas_call x1, Pallas kernels, on_device(): pl.pallas_call(functools.partial(step_kernel, n, nx, nc, chunks), out_sha...  41.9 us
    sub x1, other arithmetic, on_device(): return (latent + delta[0], latent - delta[1])  1.32 us

profile of v5, /device:TPU:0, one launch (start us, length us, event | category | flops | bytes accessed | tf_op | source)
XLA Modules:
  0.0 45.8 jit_solution(5915513789285699065)
XLA Ops:
  2.6 0.0 copy-start
  2.6 41.9 %shard_map.113 = f32[2,10,128]{2,1,0:T(8,128)} custom-call(s32[1]{0:T(128)S(6)} %copy.12.len_ref, s32[1]{0:T(128)S(6)} %copy.13.step_ref, f32[1]{0:T(128)S(6)} %copy.14.guide_ref, bf16[1,40,4096]{2,1,0:T(8,128)(2,1)} %q_ref.1, bf16[1,40,4096]{2,1,0:T(8,128)(2,1)} %k_ref.1, bf16[1,40,4096]{2,1,0:T(8,128)(2,1)} %v_ref.1, bf16[1,256,4096]{2,1,0:T(8,128)(2,1)} %rk_ref.1, ...), custom_call_target="tpu_custom_call" | custom-call | flops 880803840 | bytes 4194304 | tf_op jit(solution)/shard_map/pallas_call | solution.py:496
  44.5 0.0 copy-done
  44.5 1.3 %bitcast_subtract_fusion = (f32[10,128]{1,0:T(8,128)}, f32[10,128]{1,0:T(8,128)}) fusion(f32[10,128]{1,0:T(8,128)S(1)} %copy-done, f32[2,10,128]{2,1,0:T(8,128)} %shard_map.113), kind=kLoop, calls=%fused_computation | loop fusion | flops 2560 | bytes 25600 | tf_op jit(solution)/shard_map/sub | solution.py:540
Async XLA Ops:
  2.6 41.9 %copy-start = (f32[10,128]{1,0:T(8,128)S(1)}, f32[10,128]{1,0:T(8,128)}, u32[]{:S(2)}) copy-start(f32[10,128]{1,0:T(8,128)} %param.18) | copy-start | bytes 15364
